TPU v7x, 32 devices: a whole 2x2x4 slice. The times are simulated.
32 devices in a mesh: cube: 8 (over z, y), pair: 4 (over x, core).
Axes of the slice: x: 2, y: 2, z: 4, core: 2. Of those that a mesh axis runs over, the one named last changes fastest.
Arguments:
- own_partial: float32 [3, 2048, 512], P(None, 'cube'), may hold values from -6 to 6
- spill_partial: float32 [3, 2048, 512], P(None, 'cube'), may hold values from -6 to 6
- spill_box: int32 [2048], P('cube'), may hold values from 0 to 255, as said below
- sources: int32 [2048, 189], P('cube'), may hold values from 0 to 2047, as said below
- reflections: int32 [2048, 189], P('cube'), may hold values from 0 to 15
- operators: bfloat16 [16, 512, 512], P('pair'), may hold values from -0.01953125 to 0.01953125
Outputs:
- local_own: float32 [3, 2048, 512], P(None, 'cube', 'pair')
- local_spill: float32 [3, 2048, 512], P(None, 'cube', 'pair')
Inputs may be any that keep to these rules, and one draw needn't show every extreme that they name: The sources of box b lie on b's owner or on the owner just before or after it: from max(0, (b // 256 - 1) * 256) to min(2048, (b // 256 + 2) * 256) - 1. A source may repeat within a list. `spill_box`: the 64 entries of each aligned run of 64 are distinct.
All inputs are finite; a program needn't handle non-finite values.
Results may differ from a plain program's by a relative error of at most 0.0095.
Values may be sent and summed in bfloat16 or wider, within the bound.
A program may use at most 64 MiB of HBM per device.

v0:
```python
import jax
import jax.numpy as jnp
from jax import lax
from jax.sharding import PartitionSpec as P

SPILL = 2


def passed_along(value, axis, steps):
    count = lax.axis_size(axis)
    first, last = (max(0, -steps), min(count, count - steps))
    return lax.ppermute(value, axis, [(source, source + steps) for source in range(first, last)])


def padded(block, sides, width):
    for axis, dim in sides:
        count = lax.axis_size(axis)
        forward = [(i, i + 1) for i in range(count - 1)]
        backward = [(target, source) for source, target in forward]
        low = lax.ppermute(
            lax.slice_in_dim(block, block.shape[dim] - width, None, axis=dim), axis, forward
        )
        high = lax.ppermute(lax.slice_in_dim(block, 0, width, axis=dim), axis, backward)
        block = jnp.concatenate([low, block, high], axis=dim)
    return block


def spill_offsets():
    return [shift_by for shift_by in range(-SPILL, SPILL + 1) if shift_by != 0]


def split_pair(values):
    upper = values.astype(jnp.bfloat16)
    lower = (values - upper.astype(jnp.float32)).astype(jnp.bfloat16)
    return (upper, lower)


def split_einsum(form, exact_side, data_side):
    upper, lower = split_pair(data_side)
    first = jnp.einsum(form, exact_side, upper, preferred_element_type=jnp.float32)
    return first + jnp.einsum(form, exact_side, lower, preferred_element_type=jnp.float32)


def count_table(src_local, rel_refl, groups, extent):
    column_total = groups * extent
    low_width = 128
    high_width = (column_total + low_width - 1) // low_width
    inside = (rel_refl >= 0) & (rel_refl < groups)
    keyed = jnp.where(inside, rel_refl * extent + src_local, -1)
    high_part = jnp.where(inside, keyed // low_width, -1)
    low_part = jnp.where(inside, keyed % low_width, 0)
    high_ids = jnp.arange(high_width, dtype=jnp.int32)
    low_ids = jnp.arange(low_width, dtype=jnp.int32)
    high_onehot = (high_part[:, :, None] == high_ids).astype(jnp.bfloat16)
    low_onehot = (low_part[:, :, None] == low_ids).astype(jnp.bfloat16)
    counter = jnp.einsum(
        "tjh,tjl->thl", high_onehot, low_onehot, preferred_element_type=jnp.float32
    )
    counter = counter.reshape(keyed.shape[0], high_width * low_width)
    return counter.astype(jnp.bfloat16)


def add_reflection(summed, counter, position, window, operator, reflection):
    extent = window.shape[1]
    counts = lax.dynamic_slice_in_dim(counter, position * extent, extent, 1)
    bit_ids = jnp.arange(3, dtype=jnp.int32)
    sign_factor = (1 - 2 * (jnp.right_shift(reflection, bit_ids) & 1)).astype(jnp.float32)[
        :, None, None
    ]
    applied_all = jnp.einsum("cse,ef->csf", window, operator, preferred_element_type=jnp.float32)
    applied = split_einsum("ts,csf->ctf", counts, applied_all)
    return summed + sign_factor * applied


def on_device(own_partial, spill_partial, spill_box, sources, reflections, operators):
    box_count = own_partial.shape[1]
    coeff_count = operators.shape[2]
    slot_count = spill_box.shape[0] // (2 * SPILL)
    cube_index = lax.axis_index("cube")
    multipole = own_partial
    selectors = []
    box_ids = jnp.arange(box_count, dtype=jnp.int32)[None, :]
    for group_id, offset in enumerate(spill_offsets()):
        outgoing = spill_partial[:, group_id * slot_count : (group_id + 1) * slot_count]
        labels = spill_box[group_id * slot_count : (group_id + 1) * slot_count].astype(jnp.float32)
        got_part, got_labels = passed_along((outgoing, labels), "cube", offset)
        picker = (got_labels.astype(jnp.int32)[:, None] == box_ids).astype(jnp.bfloat16)
        multipole = multipole + split_einsum("sb,cse->cbe", picker, got_part)
        selectors.append(picker)
    window = padded(multipole.astype(jnp.bfloat16), (("cube", 1),), box_count)
    extent = window.shape[1]
    src_local = sources - (cube_index - 1) * box_count
    held_count = operators.shape[0]
    leading = lax.axis_index("pair") * held_count
    counter = count_table(src_local, reflections - leading, held_count, extent)
    summed = jnp.zeros((3, box_count, coeff_count), jnp.float32)
    for position in range(held_count):
        summed = add_reflection(
            summed, counter, position, window, operators[position], leading + position
        )
    local_field = lax.psum_scatter(summed, "pair", scatter_dimension=2, tiled=True)
    returned = []
    for group_id, offset in enumerate(spill_offsets()):
        picked = split_einsum("sb,cbe->cse", selectors[group_id], local_field)
        returned.append(passed_along(picked, "cube", -offset))
    return (local_field, jnp.concatenate(returned, axis=1))


def solution(mesh):
    in_specs = (
        P(None, "cube", None),
        P(None, "cube", None),
        P("cube"),
        P("cube", None),
        P("cube", None),
        P("pair", None, None),
    )
    out_specs = (P(None, "cube", "pair"), P(None, "cube", "pair"))
    return jax.shard_map(
        on_device, mesh=mesh, in_specs=in_specs, out_specs=out_specs, check_vma=False
    )
```

profile of v0, /device:TPU:0, one launch (start us, length us, event | category | flops | bytes accessed | tf_op | source)
XLA Modules:
  0.0 156.5 jit_solution(12134377596796661954)
XLA Ops:
  7.2 2.4 %fusion.99 = (f32[3,64,512]{2,1,0:T(8,128)S(1)}, f32[3,64,512]{2,1,0:T(8,128)S(1)}, f32[3,64,512]{2,1,0:T(8,128)S(1)}, f32[3,64,512]{2,1,0:T(8,128)}) fusion(f32[3,256,512]{2,1,0:T(8,128)} %param.7), kind=kLoop, calls=%fused_computation.130 | loop fusion | bytes 3145728 | tf_op jit(solution)/shard_map/slice | solution.py:84
  9.6 4.9 %collective-permute-start.5 = (f32[3,64,512]{2,1,0:T(8,128)}, f32[3,64,512]{2,1,0:T(8,128)S(1)}, u32[]{:S(2)}, u32[]{:S(2)}) collective-permute-start(f32[3,64,512]{2,1,0:T(8,128)} %get-tuple-element.9), channel_id=1, source_target_pairs={{0,4},{4,8},{8,12},{12,16},{16,20},{20,24},{24,28},{1,5},{5,9},{9,... | collective-permute-start | bytes 1179656 | tf_op jit(solution)/shard_map/ppermute | solution.py:12
  15.9 1.3 collective-permute-start.1
  17.2 1.3 collective-permute-start.2
  18.5 1.3 collective-permute-start.3
  20.2 5.2 %collective-permute-start.4 = (f32[64]{0:T(128)S(1)}, f32[64]{0:T(128)S(1)}, u32[]{:S(2)}, u32[]{:S(2)}) collective-permute-start(f32[64]{0:T(128)S(1)} %get-tuple-element.15), channel_id=1, source_target_pairs={{0,4},{4,8},{8,12},{12,16},{16,20},{20,24},{24,28},{1,5},{5,9},{9,... | collective-permute-start | bytes 776 | tf_op jit(solution)/shard_map/ppermute | solution.py:12
  25.4 6.5 %collective-permute-start.6 = (f32[64]{0:T(128)S(1)}, f32[64]{0:T(128)S(1)}, u32[]{:S(2)}, u32[]{:S(2)}) collective-permute-start(f32[64]{0:T(128)S(1)} %get-tuple-element.14), channel_id=1, source_target_pairs={{0,8},{4,12},{8,16},{12,20},{16,24},{20,28},{1,9},{5,13},{9,17},{1... | collective-permute-start | bytes 776 | tf_op jit(solution)/shard_map/ppermute | solution.py:12
  32.0 4.0 %collective-permute-start.7 = (f32[3,64,512]{2,1,0:T(8,128)S(1)}, f32[3,64,512]{2,1,0:T(8,128)S(1)}, u32[]{:S(2)}, u32[]{:S(2)}) collective-permute-start(f32[3,64,512]{2,1,0:T(8,128)S(1)} %get-tuple-element.8), channel_id=1, source_target_pairs={{0,8},{4,12},{8,16},{12,20},{16,24},{20,28},{1,9},{5,13},{9,17},{1... | collective-permute-start | bytes 1179656 | tf_op jit(solution)/shard_map/ppermute | solution.py:12
  38.9 3.3 %collective-permute-done.7 = f32[3,64,512]{2,1,0:T(8,128)S(1)} collective-permute-done((f32[3,64,512]{2,1,0:T(8,128)S(1)}, f32[3,64,512]{2,1,0:T(8,128)S(1)}, u32[]{:S(2)}, u32[]{:S(2)}) %collective-permute-start.7) | collective-permute-done | bytes 393248 | tf_op jit(solution)/shard_map/ppermute | solution.py:12
  42.6 1.3 fusion.9
  44.0 5.3 %collective-permute-start.8 = (bf16[3,256,512]{2,1,0:T(8,128)(2,1)S(1)}, bf16[3,256,512]{2,1,0:T(8,128)(2,1)}, u32[]{:S(2)}, u32[]{:S(2)}) collective-permute-start(bf16[3,256,512]{2,1,0:T(8,128)(2,1)S(1)} %fusion.9), channel_id=1, source_target_pairs={{0,4},{4,8},{8,12},{12,16},{16,20},{20,24},{24,28},{1,5},{5,9},{9,... | collective-permute-start | bytes 2359304 | tf_op jit(solution)/shard_map/ppermute | solution.py:20
  51.6 12.9 %fusion.7 = bf16[256,24,128]{2,1,0:T(8,128)(2,1)S(1)} fusion(s32[256,189]{1,0:T(8,128)S(1)} %copy.9, pred[256,189,24]{1,2,0:T(8,128)(4,1)S(1)} %iota_compare_fusion.18), kind=kOutput, calls=%fused_computation.14 | convolution fusion | flops 304250880 | bytes 2927616 | tf_op jit(solution)/shard_map/tjh,tjl->thl/dot_general | solution.py:56
  64.8 12.6 %collective-permute-done.8 = bf16[3,256,512]{2,1,0:T(8,128)(2,1)} collective-permute-done((bf16[3,256,512]{2,1,0:T(8,128)(2,1)S(1)}, bf16[3,256,512]{2,1,0:T(8,128)(2,1)}, u32[]{:S(2)}, u32[]{:S(2)}) %collective-permute-start.8) | collective-permute-done | bytes 786464 | tf_op jit(solution)/shard_map/ppermute | solution.py:20
  77.4 2.9 %fusion.34 = f32[3,768,512]{2,1,0:T(8,128)S(1)} fusion(bf16[4,512,512]{2,1,0:T(8,128)(2,1)} %param.11, bf16[3,256,512]{2,1,0:T(8,128)(2,1)} %collective-permute-done.9, bf16[3,256,512]{2,1,0:T(8,128)(2,1)S(1)} %fusion.9, bf16[3,256,512]{2,1,0:T(8,128)(2,1)} %collective-permute-done.8), kind=kOutput, calls=%fused_computation.51 | convolution fusion | flops 1215037440 | bytes 7602176 | tf_op jit(solution)/shard_map/cse,ef->csf/dot_general | solution.py:70
  82.8 2.8 %fusion.32 = f32[3,768,512]{2,1,0:T(8,128)S(1)} fusion(bf16[4,512,512]{2,1,0:T(8,128)(2,1)S(1)} %copy-done.5, bf16[3,256,512]{2,1,0:T(8,128)(2,1)} %collective-permute-done.9, bf16[3,256,512]{2,1,0:T(8,128)(2,1)S(1)} %fusion.9, bf16[3,256,512]{2,1,0:T(8,128)(2,1)} %collective-permute-done.8), kind=kOutput, calls=%fused_computation.49 | convolution fusion | flops 1215037440 | bytes 7602176 | tf_op jit(solution)/shard_map/cse,ef->csf/dot_general | solution.py:70
  87.3 2.8 %fusion.30 = f32[3,768,512]{2,1,0:T(8,128)S(1)} fusion(bf16[4,512,512]{2,1,0:T(8,128)(2,1)S(1)} %copy-done.5, bf16[3,256,512]{2,1,0:T(8,128)(2,1)} %collective-permute-done.9, bf16[3,256,512]{2,1,0:T(8,128)(2,1)S(1)} %fusion.9, bf16[3,256,512]{2,1,0:T(8,128)(2,1)} %collective-permute-done.8), kind=kOutput, calls=%fused_computation.47 | convolution fusion | flops 1215037440 | bytes 7602176 | tf_op jit(solution)/shard_map/cse,ef->csf/dot_general | solution.py:70
  91.9 2.8 %fusion.28 = f32[3,768,512]{2,1,0:T(8,128)S(1)} fusion(bf16[4,512,512]{2,1,0:T(8,128)(2,1)S(1)} %copy-done.5, bf16[3,256,512]{2,1,0:T(8,128)(2,1)} %collective-permute-done.9, bf16[3,256,512]{2,1,0:T(8,128)(2,1)S(1)} %fusion.9, bf16[3,256,512]{2,1,0:T(8,128)(2,1)} %collective-permute-done.8), kind=kOutput, calls=%fused_computation.45 | convolution fusion | flops 1215037440 | bytes 7602176 | tf_op jit(solution)/shard_map/cse,ef->csf/dot_general | solution.py:70
  95.5 2.9 %add_bitcast_fusion = f32[3,256,512]{1,2,0:T(8,128)} fusion(f32[3,512,256]{2,1,0:T(8,128)S(1)} %fusion.6, f32[3,512,256]{2,1,0:T(8,128)S(1)} %fusion.16, f32[3,512,256]{2,1,0:T(8,128)S(1)} %fusion.5, f32[3,512,256]{2,1,0:T(8,128)S(1)} %fusion.19, f32[3,512,256]{2,1,0:T(8,128)S(1)} %fusion.4, f32[3,512,256]{2,1,0:T(8,128)S(1)} %fusion.22, ...), kind=kOutput, calls=%fused_computation.25 | convolution fusion | flops 609484800 | bytes 17696768 | tf_op jit(solution)/shard_map/ts,csf->ctf/dot_general | solution.py:40
  98.4 31.4 %reduce-scatter.2.cloned.1.call-done = f32[3,256,128]{1,2,0:T(8,128)} async-done(((f32[3,256,512]{1,2,0:T(8,128)}), f32[3,256,128]{1,2,0:T(8,128)}) %reduce-scatter.2.cloned.1.call-update) | async-done | bytes 393232 | tf_op jit(solution)/shard_map/reduce_scatter | solution.py:101
  132.1 3.4 %collective-permute-start.10 = (f32[3,64,128]{2,1,0:T(8,128)S(1)}, f32[3,64,128]{2,1,0:T(8,128)S(1)}, u32[]{:S(2)}, u32[]{:S(2)}) collective-permute-start(f32[3,64,128]{2,1,0:T(8,128)S(1)} %fusion.27), channel_id=1, source_target_pairs={{0,8},{4,12},{8,16},{12,20},{16,24},{20,28},{1,9},{5,13},{9,17},{1... | collective-permute-start | bytes 294920 | tf_op jit(solution)/shard_map/ppermute | solution.py:12
  135.7 3.4 %collective-permute-start.11 = (f32[3,64,128]{2,1,0:T(8,128)S(1)}, f32[3,64,128]{2,1,0:T(8,128)S(1)}, u32[]{:S(2)}, u32[]{:S(2)}) collective-permute-start(f32[3,64,128]{2,1,0:T(8,128)S(1)} %fusion.26), channel_id=1, source_target_pairs={{0,4},{4,8},{8,12},{12,16},{16,20},{20,24},{24,28},{1,5},{5,9},{9,... | collective-permute-start | bytes 294920 | tf_op jit(solution)/shard_map/ppermute | solution.py:12
  139.3 1.3 collective-permute-start.12
  143.0 2.8 %collective-permute-done.12 = f32[3,64,128]{2,1,0:T(8,128)S(1)} collective-permute-done((f32[3,64,128]{2,1,0:T(8,128)S(1)}, f32[3,64,128]{2,1,0:T(8,128)S(1)}, u32[]{:S(2)}, u32[]{:S(2)}) %collective-permute-start.12) | collective-permute-done | bytes 98336 | tf_op jit(solution)/shard_map/ppermute | solution.py:12
  145.8 3.0 %collective-permute-done.13 = f32[3,64,128]{2,1,0:T(8,128)S(1)} collective-permute-done((f32[3,64,128]{2,1,0:T(8,128)S(1)}, f32[3,64,128]{2,1,0:T(8,128)S(1)}, u32[]{:S(2)}, u32[]{:S(2)}) %collective-permute-start.13) | collective-permute-done | bytes 98336 | tf_op jit(solution)/shard_map/ppermute | solution.py:12
  (64 shorter events, 20.3 us)
Async XLA Ops:
  7.2 7.4 %copy-start.4 = (s32[256]{0:T(256)S(1)}, s32[256]{0:T(256)}, u32[]{:S(2)}) copy-start(s32[256]{0:T(256)} %param.8) | copy-start | bytes 3076
  7.2 12.6 %copy-start.3 = (s32[256,189]{0,1:T(8,128)S(1)}, s32[256,189]{0,1:T(8,128)}, u32[]{:S(2)}) copy-start(s32[256,189]{0,1:T(8,128)} %param.10) | copy-start | bytes 580612
  7.2 12.6 %copy-start.2 = (s32[256,189]{0,1:T(8,128)S(1)}, s32[256,189]{0,1:T(8,128)}, u32[]{:S(2)}) copy-start(s32[256,189]{0,1:T(8,128)} %param.9) | copy-start | bytes 580612
  7.2 122.6 %reduce-scatter.2.cloned.1.call-start = ((), (), s32[]{:S(2)}) async-start(), calls=%async_computation.1 | async-start | bytes 1966080 | tf_op jit(solution)/shard_map/reduce_scatter | solution.py:101
  9.6 26.3 %collective-permute-start.5 = (f32[3,64,512]{2,1,0:T(8,128)}, f32[3,64,512]{2,1,0:T(8,128)S(1)}, u32[]{:S(2)}, u32[]{:S(2)}) collective-permute-start(f32[3,64,512]{2,1,0:T(8,128)} %get-tuple-element.9), channel_id=1, source_target_pairs={{0,4},{4,8},{8,12},{12,16},{16,20},{20,24},{24,28},{1,5},{5,9},{9,... | collective-permute-start | bytes 1179656 | tf_op jit(solution)/shard_map/ppermute | solution.py:12
  14.6 5.6 %collective-permute-start = (f32[64]{0:T(128)S(1)}, f32[64]{0:T(128)S(1)}, u32[]{:S(2)}, u32[]{:S(2)}) collective-permute-start(f32[64]{0:T(128)S(1)} %get-tuple-element.12), channel_id=1, source_target_pairs={{8,0},{12,4},{16,8},{20,12},{24,16},{28,20},{9,1},{13,5},{17,9},{2... | collective-permute-start | bytes 776 | tf_op jit(solution)/shard_map/ppermute | solution.py:12
  15.9 22.0 %collective-permute-start.1 = (f32[3,64,512]{2,1,0:T(8,128)S(1)}, f32[3,64,512]{2,1,0:T(8,128)S(1)}, u32[]{:S(2)}, u32[]{:S(2)}) collective-permute-start(f32[3,64,512]{2,1,0:T(8,128)S(1)} %get-tuple-element.6), channel_id=1, source_target_pairs={{8,0},{12,4},{16,8},{20,12},{24,16},{28,20},{9,1},{13,5},{17,9},{2... | collective-permute-start | bytes 1179656 | tf_op jit(solution)/shard_map/ppermute | solution.py:12
  17.2 8.2 %collective-permute-start.2 = (f32[64]{0:T(128)S(1)}, f32[64]{0:T(128)S(1)}, u32[]{:S(2)}, u32[]{:S(2)}) collective-permute-start(f32[64]{0:T(128)S(1)} %get-tuple-element.13), channel_id=1, source_target_pairs={{4,0},{8,4},{12,8},{16,12},{20,16},{24,20},{28,24},{5,1},{9,5},{13... | collective-permute-start | bytes 776 | tf_op jit(solution)/shard_map/ppermute | solution.py:12
  18.5 18.4 %collective-permute-start.3 = (f32[3,64,512]{2,1,0:T(8,128)S(1)}, f32[3,64,512]{2,1,0:T(8,128)S(1)}, u32[]{:S(2)}, u32[]{:S(2)}) collective-permute-start(f32[3,64,512]{2,1,0:T(8,128)S(1)} %get-tuple-element.7), channel_id=1, source_target_pairs={{4,0},{8,4},{12,8},{16,12},{20,16},{24,20},{28,24},{5,1},{9,5},{13... | collective-permute-start | bytes 1179656 | tf_op jit(solution)/shard_map/ppermute | solution.py:12
  20.2 11.8 %collective-permute-start.4 = (f32[64]{0:T(128)S(1)}, f32[64]{0:T(128)S(1)}, u32[]{:S(2)}, u32[]{:S(2)}) collective-permute-start(f32[64]{0:T(128)S(1)} %get-tuple-element.15), channel_id=1, source_target_pairs={{0,4},{4,8},{8,12},{12,16},{16,20},{20,24},{24,28},{1,5},{5,9},{9,... | collective-permute-start | bytes 776 | tf_op jit(solution)/shard_map/ppermute | solution.py:12
  25.4 10.5 %collective-permute-start.6 = (f32[64]{0:T(128)S(1)}, f32[64]{0:T(128)S(1)}, u32[]{:S(2)}, u32[]{:S(2)}) collective-permute-start(f32[64]{0:T(128)S(1)} %get-tuple-element.14), channel_id=1, source_target_pairs={{0,8},{4,12},{8,16},{12,20},{16,24},{20,28},{1,9},{5,13},{9,17},{1... | collective-permute-start | bytes 776 | tf_op jit(solution)/shard_map/ppermute | solution.py:12
  32.0 10.2 %collective-permute-start.7 = (f32[3,64,512]{2,1,0:T(8,128)S(1)}, f32[3,64,512]{2,1,0:T(8,128)S(1)}, u32[]{:S(2)}, u32[]{:S(2)}) collective-permute-start(f32[3,64,512]{2,1,0:T(8,128)S(1)} %get-tuple-element.8), channel_id=1, source_target_pairs={{0,8},{4,12},{8,16},{12,20},{16,24},{20,28},{1,9},{5,13},{9,17},{1... | collective-permute-start | bytes 1179656 | tf_op jit(solution)/shard_map/ppermute | solution.py:12
  38.4 4.3 %copy-start.1 = (f32[3,256,512]{2,1,0:T(8,128)S(1)}, f32[3,256,512]{2,1,0:T(8,128)}, u32[]{:S(2)}) copy-start(f32[3,256,512]{2,1,0:T(8,128)} %param.6) | copy-start | bytes 4718596
  44.0 33.4 %collective-permute-start.8 = (bf16[3,256,512]{2,1,0:T(8,128)(2,1)S(1)}, bf16[3,256,512]{2,1,0:T(8,128)(2,1)}, u32[]{:S(2)}, u32[]{:S(2)}) collective-permute-start(bf16[3,256,512]{2,1,0:T(8,128)(2,1)S(1)} %fusion.9), channel_id=1, source_target_pairs={{0,4},{4,8},{8,12},{12,16},{16,20},{20,24},{24,28},{1,5},{5,9},{9,... | collective-permute-start | bytes 2359304 | tf_op jit(solution)/shard_map/ppermute | solution.py:20
  49.3 28.1 %collective-permute-start.9 = (bf16[3,256,512]{2,1,0:T(8,128)(2,1)S(1)}, bf16[3,256,512]{2,1,0:T(8,128)(2,1)}, u32[]{:S(2)}, u32[]{:S(2)}) collective-permute-start(bf16[3,256,512]{2,1,0:T(8,128)(2,1)S(1)} %fusion.9), channel_id=1, source_target_pairs={{4,0},{8,4},{12,8},{16,12},{20,16},{24,20},{28,24},{5,1},{9,5},{13... | collective-permute-start | bytes 2359304 | tf_op jit(solution)/shard_map/ppermute | solution.py:23
  81.2 1.6 %copy-start.5 = (bf16[4,512,512]{2,1,0:T(8,128)(2,1)S(1)}, bf16[4,512,512]{2,1,0:T(8,128)(2,1)}, u32[]{:S(2)}) copy-start(bf16[4,512,512]{2,1,0:T(8,128)(2,1)} %param.11) | copy-start | bytes 6291460
  129.8 12.3 %copy-start = (f32[3,256,128]{1,2,0:T(8,128)S(1)}, f32[3,256,128]{1,2,0:T(8,128)}, u32[]{:S(2)}) copy-start(f32[3,256,128]{1,2,0:T(8,128)} %reduce-scatter.2.cloned.1.call-done) | copy-start | bytes 1179652
  132.1 10.9 %collective-permute-start.10 = (f32[3,64,128]{2,1,0:T(8,128)S(1)}, f32[3,64,128]{2,1,0:T(8,128)S(1)}, u32[]{:S(2)}, u32[]{:S(2)}) collective-permute-start(f32[3,64,128]{2,1,0:T(8,128)S(1)} %fusion.27), channel_id=1, source_target_pairs={{0,8},{4,12},{8,16},{12,20},{16,24},{20,28},{1,9},{5,13},{9,17},{1... | collective-permute-start | bytes 294920 | tf_op jit(solution)/shard_map/ppermute | solution.py:12
  135.7 7.3 %collective-permute-start.11 = (f32[3,64,128]{2,1,0:T(8,128)S(1)}, f32[3,64,128]{2,1,0:T(8,128)S(1)}, u32[]{:S(2)}, u32[]{:S(2)}) collective-permute-start(f32[3,64,128]{2,1,0:T(8,128)S(1)} %fusion.26), channel_id=1, source_target_pairs={{0,4},{4,8},{8,12},{12,16},{16,20},{20,24},{24,28},{1,5},{5,9},{9,... | collective-permute-start | bytes 294920 | tf_op jit(solution)/shard_map/ppermute | solution.py:12
  139.3 6.5 %collective-permute-start.12 = (f32[3,64,128]{2,1,0:T(8,128)S(1)}, f32[3,64,128]{2,1,0:T(8,128)S(1)}, u32[]{:S(2)}, u32[]{:S(2)}) collective-permute-start(f32[3,64,128]{2,1,0:T(8,128)S(1)} %fusion.25), channel_id=1, source_target_pairs={{4,0},{8,4},{12,8},{16,12},{20,16},{24,20},{28,24},{5,1},{9,5},{13... | collective-permute-start | bytes 294920 | tf_op jit(solution)/shard_map/ppermute | solution.py:12
  140.8 8.0 %collective-permute-start.13 = (f32[3,64,128]{2,1,0:T(8,128)S(1)}, f32[3,64,128]{2,1,0:T(8,128)S(1)}, u32[]{:S(2)}, u32[]{:S(2)}) collective-permute-start(f32[3,64,128]{2,1,0:T(8,128)S(1)} %fusion.24), channel_id=1, source_target_pairs={{8,0},{12,4},{16,8},{20,12},{24,16},{28,20},{9,1},{13,5},{17,9},{2... | collective-permute-start | bytes 294920 | tf_op jit(solution)/shard_map/ppermute | solution.py:12
Sparse Core Ops, SparseCore 0:
  98.6 31.1 reduce-scatter.1
where the time goes:
time: 157 us; the launch traced here: 156 us
  waiting for transfers between devices  53.1 us (34%)
  starting transfers between devices  41.7 us (27%)
  matrix products  39.4 us (25%)
  between operations  14.5 us (9%)
  local copies, waits for them, and re-layouts  4.61 us (3%)
  other arithmetic  3.22 us (2%)
    ppermute x12, starting transfers between devices, passed_along(): lax.ppermute(value, axis, [(source, source + steps) for source in range(f...  35.1 us
    reduce_scatter x1, waiting for transfers between devices, on_device(): lax.psum_scatter(summed, 'pair', scatter_dimension=2, tiled=True)  31.4 us
    dot_general x1, matrix products, count_table(): jnp.einsum('tjh,tjl->thl', high_onehot, low_onehot, preferred_element_typ...  12.9 us
    ppermute x1, waiting for transfers between devices, padded(): lax.ppermute(lax.slice_in_dim(block, block.shape[dim] - width, None, axis...  12.6 us
    dot_general x4, matrix products, add_reflection(): jnp.einsum('cse,ef->csf', window, operator, preferred_element_type=jnp.fl...  11.3 us
    ppermute x12, waiting for transfers between devices, passed_along(): lax.ppermute(value, axis, [(source, source + steps) for source in range(f...  9.12 us
    dot_general x12, matrix products, split_einsum(): jnp.einsum(form, exact_side, upper, preferred_element_type=jnp.float32)  8.2 us
    dot_general x12, matrix products, split_einsum(): jnp.einsum(form, exact_side, lower, preferred_element_type=jnp.float32)  6.97 us
  transfers between devices with their start and end apart: 15, of which 5 were waited for; matrix products, arithmetic and copies ran while one was open for 12% of the time, Pallas kernels for 0%

commit v1 on v0

v1 whole, which is shorter than its diff:
```python
import functools

import jax
import jax.numpy as jnp
from jax import lax
from jax.experimental import pallas as pl
from jax.experimental.pallas import tpu as pltpu
from jax.sharding import PartitionSpec as P

SPILL = 2
LOW, OWN, HIGH = 0, 1, 2
LANES = 128
BF = jnp.bfloat16
F32 = jnp.float32


def shifts():
    return [k for k in range(-SPILL, SPILL + 1) if k != 0]


def kernel(
    cubes, pairs,
    own_hbm, spill_hbm, box_ref, src_ref, refl_ref, op_hbm,
    own_out, spill_out,
    own_v, spill_v, op_v, lab_send, lab_recv, sp_send, sp_recv,
    key_hi, key_lo, cnt_f, cnt, win, mixed, part, rs1_send, rs1_recv, rs2_send, rs2_recv,
    field, rt_send, rt_recv,
    local_sem, lab_sem, sp_sem, halo_sem, far_sem, near_sem, rs1_sem, rs2_sem, rt_sem,
):
    c = lax.axis_index("cube")
    p = lax.axis_index("pair")
    half = pairs // 2
    far = lax.rem(p + half, pairs)
    near = p + 1 - 2 * lax.rem(p, 2)
    hi, lo = p // 2, lax.rem(p, 2)
    comps, boxes, q = own_v.shape
    held, coeffs, outs = op_v.shape
    slots = sp_send.shape[1]
    extent = 3 * boxes
    tiles = extent // LANES
    rows = cnt_f.shape[0] // boxes
    entries = src_ref.shape[1]

    def inside(k):
        return (c + k >= 0) & (c + k < cubes)

    def remote(src, dst, sems, **where):
        return pltpu.make_async_remote_copy(
            src_ref=src, dst_ref=dst, send_sem=sems.at[0], recv_sem=sems.at[1],
            device_id=where, device_id_type=pl.DeviceIdType.MESH,
        )

    barrier = pltpu.get_barrier_semaphore()
    partners = 2
    for other in (far, near):
        pl.semaphore_signal(barrier, inc=1, device_id={"pair": other}, device_id_type=pl.DeviceIdType.MESH)
    for k in shifts():
        partners = partners + inside(k).astype(jnp.int32)

        @pl.when(inside(k))
        def _():
            pl.semaphore_signal(barrier, inc=1, device_id={"cube": c + k}, device_id_type=pl.DeviceIdType.MESH)

    mine = pl.ds(pl.multiple_of(p * q, q), q)
    read_spill = pltpu.make_async_copy(spill_hbm.at[:, :, mine], spill_v, local_sem.at[0])
    read_own = pltpu.make_async_copy(own_hbm.at[:, :, mine], own_v, local_sem.at[1])
    read_op = pltpu.make_async_copy(op_hbm, op_v, local_sem.at[2])
    read_spill.start()
    read_own.start()
    read_op.start()

    groups = list(enumerate(shifts()))
    for g, k in groups:
        lab_send[g, 0:1, 0:slots] = box_ref[0:1, g * slots:(g + 1) * slots]
    read_spill.wait()
    for g, k in groups:
        for m in range(comps):
            sp_send[g, :, m * q:(m + 1) * q] = spill_v[m, g * slots:(g + 1) * slots, :].astype(BF)
    pl.semaphore_wait(barrier, partners)

    def send_spill(g, k):
        return remote(sp_send.at[g], sp_recv.at[g], sp_sem.at[g], cube=c + k)

    def send_label(g, k):
        return remote(lab_send.at[g], lab_recv.at[g], lab_sem.at[g], cube=c + k)

    for g, k in groups:
        @pl.when(inside(k))
        def _(g=g, k=k):
            send_spill(g, k).start()
            send_label(g, k).start()

    rel = refl_ref[...] - p * held
    ok = (rel >= 0) & (rel < held)
    key = rel * extent + src_ref[...] - (c - 1) * boxes
    key_hi[...] = jnp.full(key_hi.shape, -1.0, F32)
    key_lo[...] = jnp.zeros(key_lo.shape, F32)
    key_hi[:, 0:entries] = jnp.where(ok, lax.shift_right_arithmetic(key, 7), -1).astype(F32)
    key_lo[:, 0:entries] = jnp.where(ok, key & (LANES - 1), 0).astype(F32)

    width = key_hi.shape[1]
    ids_hi = lax.broadcasted_iota(jnp.int32, (rows, width), 0).astype(F32).astype(BF)
    ids_lo = lax.broadcasted_iota(jnp.int32, (LANES, width), 0).astype(F32).astype(BF)
    one, zero = jnp.ones((), BF), jnp.zeros((), BF)

    def count(step, carry):
        base = pl.multiple_of(step * 8, 8)
        his = key_hi[pl.ds(base, 8), :]
        los = key_lo[pl.ds(base, 8), :]
        for u in range(8):
            a = jnp.where(his[u:u + 1].astype(BF) == ids_hi, one, zero)
            b = jnp.where(los[u:u + 1].astype(BF) == ids_lo, one, zero)
            got = lax.dot_general(a, b, (((1,), (1,)), ((), ())), preferred_element_type=F32)
            cnt_f[pl.ds(pl.multiple_of((base + u) * rows, rows), rows), :] = got
        return carry

    steps = boxes // 8
    lax.fori_loop(0, steps // 2, count, 0)

    read_own.wait()
    box_ids = lax.broadcasted_iota(jnp.int32, (boxes, slots), 0)

    def picker(g):
        return jnp.where(lab_recv[g, 0:1, 0:slots] == box_ids, 1.0, 0.0).astype(BF)

    for g, k in groups:
        @pl.when(inside(-k))
        def _(g=g, k=k):
            send_spill(g, k).wait_recv()
            send_label(g, k).wait_recv()
            more = jnp.dot(picker(g), sp_recv[g], preferred_element_type=F32)
            for m in range(comps):
                own_v[m] += more[:, m * q:(m + 1) * q]

    for m in range(comps):
        win[p, OWN, m] = own_v[m].astype(BF)

    def up(m):
        return remote(win.at[p, OWN, m], win.at[p, LOW, m], halo_sem.at[0, m], cube=c + 1)

    def down(m):
        return remote(win.at[p, OWN, m], win.at[p, HIGH, m], halo_sem.at[1, m], cube=c - 1)

    def to_far(b, m):
        return remote(win.at[p, b, m], win.at[p, b, m], far_sem.at[b, m], pair=far)

    def to_near(b, m, which):
        owner = (p, far)[which]
        return remote(win.at[owner, b, m], win.at[owner, b, m], near_sem.at[which, b, m], pair=near)

    for m in range(comps):
        @pl.when(inside(1))
        def _():
            up(m).start()

        @pl.when(inside(-1))
        def _():
            down(m).start()

        to_far(OWN, m).start()
        to_near(OWN, m, 0).start()

    @pl.when(jnp.logical_not(inside(-1)))
    def _():
        win[p, LOW] = jnp.zeros(win.shape[2:], BF)

    @pl.when(jnp.logical_not(inside(1)))
    def _():
        win[p, HIGH] = jnp.zeros(win.shape[2:], BF)

    lax.fori_loop(steps // 2, steps, count, 0)

    def relay(m):
        @pl.when(inside(-1))
        def _():
            up(m).wait_recv()

        to_far(LOW, m).start()
        to_near(LOW, m, 0).start()

        @pl.when(inside(1))
        def _():
            down(m).wait_recv()

        to_far(HIGH, m).start()
        to_near(HIGH, m, 0).start()
        to_far(OWN, m).wait_recv()
        to_near(OWN, m, 1).start()

    def pass_near(m):
        for b in (LOW, HIGH):
            to_far(b, m).wait_recv()
            to_near(b, m, 1).start()

    def reduce_near(m):
        return remote(rs1_send.at[m], rs1_recv.at[m], rs1_sem.at[m], pair=near)

    def reduce_far(m):
        return remote(rs2_send.at[m], rs2_recv.at[m], rs2_sem.at[m], pair=far)

    def columns(index):
        return pl.ds(pl.multiple_of(index * q, q), q)

    def compute(m):
        for b in (LOW, OWN, HIGH):
            for which in range(2):
                to_near(b, m, which).wait_recv()
        window = jnp.concatenate(
            [jnp.concatenate([win[s, b, m] for s in range(pairs)], axis=1) for b in (LOW, OWN, HIGH)],
            axis=0,
        )
        for r in range(held):
            sign = 1 - 2 * (lax.shift_right_logical(p * held + r, m) & 1)
            summed = jnp.dot(cnt[r * boxes:(r + 1) * boxes, :], window, preferred_element_type=F32)
            mixed[:, r * coeffs:(r + 1) * coeffs] = (summed * sign.astype(F32)).astype(BF)
        part[m] = jnp.dot(
            mixed[...], op_v[...].reshape(held * coeffs, outs), preferred_element_type=F32
        )
        for h in range(half):
            rs1_send[m, h] = part[m, :, columns(2 * h + 1 - lo)].astype(BF)
        reduce_near(m).start()

    def fold(m):
        reduce_near(m).wait_recv()
        there = far // 2
        rs2_send[m] = (part[m, :, columns(far)] + rs1_recv[m, there].astype(F32)).astype(BF)
        reduce_far(m).start()

    def finish(m):
        reduce_far(m).wait_recv()
        total = part[m, :, columns(p)] + rs1_recv[m, hi].astype(F32) + rs2_recv[m].astype(F32)
        own_out[m] = total
        field[:, m * q:(m + 1) * q] = total.astype(BF)

    relay(0)
    for r in range(held):
        for t in range(tiles):
            cnt[r * boxes:(r + 1) * boxes, t * LANES:(t + 1) * LANES] = cnt_f[
                pl.ds(r * tiles + t, boxes, stride=rows), :
            ].astype(BF)
    relay(1)
    pass_near(0)
    relay(2)
    pass_near(1)
    read_op.wait()
    compute(0)
    pass_near(2)
    compute(1)
    fold(0)
    compute(2)
    fold(1)
    finish(0)
    fold(2)
    finish(1)
    finish(2)

    def send_back(g, k):
        return remote(rt_send.at[g], rt_recv.at[g], rt_sem.at[g], cube=c - k)

    for g, k in groups:
        @pl.when(inside(-k))
        def _(g=g, k=k):
            rt_send[g] = lax.dot_general(
                picker(g), field[...], (((0,), (0,)), ((), ())), preferred_element_type=F32
            ).astype(BF)
            send_back(g, k).start()

    for g, k in groups:
        rows_out = slice(g * slots, (g + 1) * slots)

        @pl.when(inside(k))
        def _(g=g, k=k, rows_out=rows_out):
            send_back(g, k).wait_recv()
            for m in range(comps):
                spill_out[m, rows_out, :] = rt_recv[g, :, m * q:(m + 1) * q].astype(F32)

        @pl.when(jnp.logical_not(inside(k)))
        def _(rows_out=rows_out):
            for m in range(comps):
                spill_out[m, rows_out, :] = jnp.zeros((slots, q), F32)

    for g, k in groups:
        @pl.when(inside(k))
        def _(g=g, k=k):
            send_spill(g, k).wait_send()
            send_label(g, k).wait_send()

        @pl.when(inside(-k))
        def _(g=g, k=k):
            send_back(g, k).wait_send()

    for m in range(comps):
        @pl.when(inside(1))
        def _(m=m):
            up(m).wait_send()

        @pl.when(inside(-1))
        def _(m=m):
            down(m).wait_send()

        for b in (LOW, OWN, HIGH):
            to_far(b, m).wait_send()
            to_near(b, m, 0).wait_send()
            to_near(b, m, 1).wait_send()
        reduce_near(m).wait_send()
        reduce_far(m).wait_send()


def on_device(cubes, pairs, own_partial, spill_partial, spill_box, sources, reflections, operators):
    comps, boxes, coeffs = own_partial.shape
    held, _, outs = operators.shape
    spills = spill_box.shape[0]
    groups = 2 * SPILL
    slots = spills // groups
    q = coeffs // pairs
    extent = 3 * boxes
    rows = -(-(held * extent // LANES) // 16) * 16
    width = -(-sources.shape[1] // LANES) * LANES
    dma = pltpu.SemaphoreType.DMA
    vmem = pl.BlockSpec(memory_space=pltpu.VMEM)
    anywhere = pl.BlockSpec(memory_space=pl.ANY)
    return pl.pallas_call(
        functools.partial(kernel, cubes, pairs),
        out_shape=(
            jax.ShapeDtypeStruct((comps, boxes, q), F32),
            jax.ShapeDtypeStruct((comps, spills, q), F32),
        ),
        in_specs=[anywhere, anywhere, vmem, vmem, vmem, anywhere],
        out_specs=(vmem, vmem),
        scratch_shapes=[
            pltpu.VMEM((comps, boxes, q), F32),
            pltpu.VMEM((comps, spills, q), F32),
            pltpu.VMEM((held, coeffs, outs), BF),
            pltpu.VMEM((groups, 8, LANES), jnp.int32),
            pltpu.VMEM((groups, 8, LANES), jnp.int32),
            pltpu.VMEM((groups, slots, comps * q), BF),
            pltpu.VMEM((groups, slots, comps * q), BF),
            pltpu.VMEM((boxes, width), F32),
            pltpu.VMEM((boxes, width), F32),
            pltpu.VMEM((boxes * rows, LANES), F32),
            pltpu.VMEM((held * boxes, extent), BF),
            pltpu.VMEM((pairs, 3, comps, boxes, q), BF),
            pltpu.VMEM((boxes, held * coeffs), BF),
            pltpu.VMEM((comps, boxes, outs), F32),
            pltpu.VMEM((comps, pairs // 2, boxes, q), BF),
            pltpu.VMEM((comps, pairs // 2, boxes, q), BF),
            pltpu.VMEM((comps, boxes, q), BF),
            pltpu.VMEM((comps, boxes, q), BF),
            pltpu.VMEM((boxes, comps * q), BF),
            pltpu.VMEM((groups, slots, comps * q), BF),
            pltpu.VMEM((groups, slots, comps * q), BF),
            dma((3,)),
            dma((groups, 2)),
            dma((groups, 2)),
            dma((2, comps, 2)),
            dma((3, comps, 2)),
            dma((2, 3, comps, 2)),
            dma((comps, 2)),
            dma((comps, 2)),
            dma((groups, 2)),
        ],
        compiler_params=pltpu.CompilerParams(
            collective_id=0, has_side_effects=True, vmem_limit_bytes=40 * 1024 * 1024
        ),
        name="far_field",
    )(own_partial, spill_partial, spill_box.reshape(1, spills), sources, reflections, operators)


def solution(mesh):
    cubes, pairs = mesh.shape["cube"], mesh.shape["pair"]
    in_specs = (
        P(None, "cube", None),
        P(None, "cube", None),
        P("cube"),
        P("cube", None),
        P("cube", None),
        P("pair", None, None),
    )
    out_specs = (P(None, "cube", "pair"), P(None, "cube", "pair"))
    return jax.shard_map(
        functools.partial(on_device, cubes, pairs),
        mesh=mesh, in_specs=in_specs, out_specs=out_specs, check_vma=False,
    )
```

time: 157 us -> 50.5 us (0.32)
  waiting for transfers between devices: 53.1 us -> 0 us
  starting transfers between devices: 41.7 us -> 0 us
  Pallas kernels: 0 us -> 40.8 us
  matrix products: 39.4 us -> 0 us
  between operations: 14.5 us -> 0.67 us
  local copies, waits for them, and re-layouts: 4.61 us -> 8.68 us
  other arithmetic: 3.22 us -> 0 us
    ppermute x14 -> x0, starting transfers between devices: 41.6 us -> none  [the longest x12 35.1 us: passed_along(): lax.ppermute(value, axis, [(source, source + steps) for source in range(f...]
    pallas_call x0 -> x1, Pallas kernels: none -> 40.8 us  [on_device(): pl.pallas_call(functools.partial(kernel, cubes, pairs), out_shape=(jax.Sh...]
    dot_general x29 -> x0, matrix products: 39.4 us -> none  [the longest x1 12.9 us: count_table(): jnp.einsum('tjh,tjl->thl', high_onehot, low_onehot, preferred_element_typ...]
    reduce_scatter x1 -> x0, waiting for transfers between devices: 31.4 us -> none  [on_device(): lax.psum_scatter(summed, 'pair', scatter_dimension=2, tiled=True)]
    ppermute x14 -> x0, waiting for transfers between devices: 21.7 us -> none  [the longest x1 12.6 us: padded(): lax.ppermute(lax.slice_in_dim(block, block.shape[dim] - width, None, axis...]
    unnamed x14 -> x12, local copies, waits for them, and re-layouts: 1.95 us -> 8.68 us
    slice x1 -> x0, local copies, waits for them, and re-layouts: 2.4 us -> none  [on_device(): spill_partial[:, group_id * slot_count:(group_id + 1) * slot_count]]
  transfers between devices with their start and end apart: 15 -> 0, of which waited for: 5 -> 0; matrix products, arithmetic and copies ran while one was open for 12% -> 0% of each run, Pallas kernels for 0% -> 0%
where the time goes in v1:
time: 50.5 us; the launch traced here: 50.2 us
  Pallas kernels  40.8 us (81%)
  local copies, waits for them, and re-layouts  8.68 us (17%)
  between operations  0.67 us (1%)
    pallas_call x1, Pallas kernels, on_device(): pl.pallas_call(functools.partial(kernel, cubes, pairs), out_shape=(jax.Sh...  40.8 us
    unnamed x12, local copies, waits for them, and re-layouts  8.68 us

profile of v1, /device:TPU:0, one launch (start us, length us, event | category | flops | bytes accessed | tf_op | source)
XLA Modules:
  0.0 50.2 jit_solution(10462688940034081759)
XLA Ops:
  0.6 1.1 %copy.8.src_ref = s32[256,189]{1,0:T(8,128)S(1)} copy(s32[256,189]{0,1:T(8,128)} %param.9) | data formatting | bytes 387072 | tf_op args[3]
  1.7 1.1 %copy.9.refl_ref = s32[256,189]{1,0:T(8,128)S(1)} copy(s32[256,189]{0,1:T(8,128)} %param.10) | data formatting | bytes 387072 | tf_op args[4]
  2.8 0.0 copy-start
  2.8 1.6 %copy-done = bf16[4,512,512]{2,1,0:T(8,128)(2,1)S(1)} copy-done((bf16[4,512,512]{2,1,0:T(8,128)(2,1)S(1)}, bf16[4,512,512]{2,1,0:T(8,128)(2,1)}, u32[]{:S(2)}) %copy-start) | copy-done | bytes 2097176
  4.4 0.0 copy-start.1
  4.4 1.4 %copy-done.1 = f32[3,256,512]{2,1,0:T(8,128)S(1)} copy-done((f32[3,256,512]{2,1,0:T(8,128)S(1)}, f32[3,256,512]{2,1,0:T(8,128)}, u32[]{:S(2)}) %copy-start.1) | copy-done | bytes 1572888
  5.8 0.0 copy-start.2
  5.8 1.4 %copy-done.2 = f32[3,256,512]{2,1,0:T(8,128)S(1)} copy-done((f32[3,256,512]{2,1,0:T(8,128)S(1)}, f32[3,256,512]{2,1,0:T(8,128)}, u32[]{:S(2)}) %copy-start.2) | copy-done | bytes 1572888
  7.2 0.0 copy-start.3
  7.2 0.7 %copy-done.3 = s32[256]{0:T(256)S(1)} copy-done((s32[256]{0:T(256)S(1)}, s32[256]{0:T(256)}, u32[]{:S(2)}) %copy-start.3) | copy-done | bytes 1048
  7.8 40.8 %far_field.1 = (f32[3,256,128]{2,1,0:T(8,128)S(1)}, f32[3,256,128]{2,1,0:T(8,128)S(1)}) custom-call(f32[3,256,512]{2,1,0:T(8,128)S(1)} %copy-done.1, f32[3,256,512]{2,1,0:T(8,128)S(1)} %copy-done.2, s32[1,256]{1,0:T(1,128)S(1)} %bitcast.1, s32[256,189]{1,0:T(8,128)S(1)} %copy.8.src_ref, s32[256,189]{1,0:T(8,128)S(1)} %copy.9.refl_ref, ...), custom_call_target="tpu_custom_call" | custom-call | tf_op jit(solution)/shard_map/far_field/pallas_call | solution.py:322
  48.7 0.7 %copy.12 = f32[3,256,128]{2,1,0:T(8,128)} copy(f32[3,256,128]{2,1,0:T(8,128)S(1)} %get-tuple-element.4) | data formatting | bytes 786432
  49.4 0.7 %copy.13 = f32[3,256,128]{2,1,0:T(8,128)} copy(f32[3,256,128]{2,1,0:T(8,128)S(1)} %get-tuple-element.5) | data formatting | bytes 786432
Async XLA Ops:
  2.8 1.6 %copy-start = (bf16[4,512,512]{2,1,0:T(8,128)(2,1)S(1)}, bf16[4,512,512]{2,1,0:T(8,128)(2,1)}, u32[]{:S(2)}) copy-start(bf16[4,512,512]{2,1,0:T(8,128)(2,1)} %op_hbm.1) | copy-start | bytes 6291460
  4.4 1.4 %copy-start.1 = (f32[3,256,512]{2,1,0:T(8,128)S(1)}, f32[3,256,512]{2,1,0:T(8,128)}, u32[]{:S(2)}) copy-start(f32[3,256,512]{2,1,0:T(8,128)} %own_hbm.1) | copy-start | bytes 4718596
  5.8 1.4 %copy-start.2 = (f32[3,256,512]{2,1,0:T(8,128)S(1)}, f32[3,256,512]{2,1,0:T(8,128)}, u32[]{:S(2)}) copy-start(f32[3,256,512]{2,1,0:T(8,128)} %spill_hbm.1) | copy-start | bytes 4718596
  7.2 0.7 %copy-start.3 = (s32[256]{0:T(256)S(1)}, s32[256]{0:T(256)}, u32[]{:S(2)}) copy-start(s32[256]{0:T(256)} %param.8) | copy-start | bytes 3076

commit v2 on v1

--- a/solution.py
+++ b/solution.py
@@ -10,6 +10,7 @@
 SPILL = 2
 LOW, OWN, HIGH = 0, 1, 2
 LANES = 128
+COUNT_CUTS = (0, 4, 8, 12, 16, 16)
 BF = jnp.bfloat16
 F32 = jnp.float32
 
@@ -20,11 +21,11 @@
 
 def kernel(
     cubes, pairs,
-    own_hbm, spill_hbm, box_ref, src_ref, refl_ref, op_hbm,
+    own_hbm, spill_hbm, box_hbm, src_hbm, refl_hbm, op_hbm,
     own_out, spill_out,
-    own_v, spill_v, op_v, lab_send, lab_recv, sp_send, sp_recv,
-    key_hi, key_lo, cnt_f, cnt, win, mixed, part, rs1_send, rs1_recv, rs2_send, rs2_recv,
-    field, rt_send, rt_recv,
+    own_v, spill_v, op_v, box_ref, src_ref, refl_ref, lab_send, lab_recv, sp_send, sp_recv,
+    keys, key_hi, key_lo, cnt_f, cnt, win, mixed, part, rs1_send, rs1_recv, rs2_send, rs2_recv,
+    pick, pick_t, rt_send, rt_recv,
     local_sem, lab_sem, sp_sem, halo_sem, far_sem, near_sem, rs1_sem, rs2_sem, rt_sem,
 ):
     c = lax.axis_index("cube")
@@ -35,11 +36,11 @@
     hi, lo = p // 2, lax.rem(p, 2)
     comps, boxes, q = own_v.shape
     held, coeffs, outs = op_v.shape
-    slots = sp_send.shape[1]
+    slots = sp_send.shape[2]
     extent = 3 * boxes
     tiles = extent // LANES
     rows = cnt_f.shape[0] // boxes
-    entries = src_ref.shape[1]
+    entries = src_ref.shape[0]
 
     def inside(k):
         return (c + k >= 0) & (c + k < cubes)
@@ -65,38 +66,53 @@
     read_spill = pltpu.make_async_copy(spill_hbm.at[:, :, mine], spill_v, local_sem.at[0])
     read_own = pltpu.make_async_copy(own_hbm.at[:, :, mine], own_v, local_sem.at[1])
     read_op = pltpu.make_async_copy(op_hbm, op_v, local_sem.at[2])
+    read_box = pltpu.make_async_copy(box_hbm, box_ref, local_sem.at[3])
+    read_src = pltpu.make_async_copy(src_hbm, src_ref, local_sem.at[4])
+    read_refl = pltpu.make_async_copy(refl_hbm, refl_ref, local_sem.at[5])
+    read_box.start()
     read_spill.start()
+    read_src.start()
+    read_refl.start()
     read_own.start()
     read_op.start()
 
     groups = list(enumerate(shifts()))
+
+    def send_spill(g, k, m):
+        return remote(sp_send.at[g, m], sp_recv.at[g, m], sp_sem.at[g, m], cube=c + k)
+
+    def send_label(g, k):
+        return remote(lab_send.at[g], lab_recv.at[g], lab_sem.at[g], cube=c + k)
+
+    read_box.wait()
     for g, k in groups:
         lab_send[g, 0:1, 0:slots] = box_ref[0:1, g * slots:(g + 1) * slots]
     read_spill.wait()
-    for g, k in groups:
-        for m in range(comps):
-            sp_send[g, :, m * q:(m + 1) * q] = spill_v[m, g * slots:(g + 1) * slots, :].astype(BF)
-    pl.semaphore_wait(barrier, partners)
-
-    def send_spill(g, k):
-        return remote(sp_send.at[g], sp_recv.at[g], sp_sem.at[g], cube=c + k)
-
-    def send_label(g, k):
-        return remote(lab_send.at[g], lab_recv.at[g], lab_sem.at[g], cube=c + k)
-
-    for g, k in groups:
-        @pl.when(inside(k))
-        def _(g=g, k=k):
-            send_spill(g, k).start()
-            send_label(g, k).start()
-
+    for m in range(comps):
+        for g, k in groups:
+            sp_send[g, m] = spill_v[m, g * slots:(g + 1) * slots, :].astype(BF)
+        if m == 0:
+            pl.semaphore_wait(barrier, partners)
+            for g, k in groups:
+                @pl.when(inside(k))
+                def _(g=g, k=k):
+                    send_label(g, k).start()
+
+        for g, k in groups:
+            @pl.when(inside(k))
+            def _(g=g, k=k, m=m):
+                send_spill(g, k, m).start()
+
+    read_src.wait()
+    read_refl.wait()
     rel = refl_ref[...] - p * held
     ok = (rel >= 0) & (rel < held)
     key = rel * extent + src_ref[...] - (c - 1) * boxes
-    key_hi[...] = jnp.full(key_hi.shape, -1.0, F32)
-    key_lo[...] = jnp.zeros(key_lo.shape, F32)
-    key_hi[:, 0:entries] = jnp.where(ok, lax.shift_right_arithmetic(key, 7), -1).astype(F32)
-    key_lo[:, 0:entries] = jnp.where(ok, key & (LANES - 1), 0).astype(F32)
+    keys[...] = jnp.full(keys.shape, -1.0, F32)
+    keys[0:entries, :] = jnp.where(ok, key, -1).astype(F32)
+    turned = jnp.transpose(keys[...]).astype(jnp.int32)
+    key_hi[...] = lax.shift_right_arithmetic(turned, 7).astype(F32)
+    key_lo[...] = (turned & (LANES - 1)).astype(F32)
 
     width = key_hi.shape[1]
     ids_hi = lax.broadcasted_iota(jnp.int32, (rows, width), 0).astype(F32).astype(BF)
@@ -104,36 +120,36 @@
     one, zero = jnp.ones((), BF), jnp.zeros((), BF)
 
     def count(step, carry):
-        base = pl.multiple_of(step * 8, 8)
-        his = key_hi[pl.ds(base, 8), :]
-        los = key_lo[pl.ds(base, 8), :]
-        for u in range(8):
+        base = pl.multiple_of(step * 16, 16)
+        his = key_hi[pl.ds(base, 16), :]
+        los = key_lo[pl.ds(base, 16), :]
+        for u in range(16):
             a = jnp.where(his[u:u + 1].astype(BF) == ids_hi, one, zero)
             b = jnp.where(los[u:u + 1].astype(BF) == ids_lo, one, zero)
             got = lax.dot_general(a, b, (((1,), (1,)), ((), ())), preferred_element_type=F32)
             cnt_f[pl.ds(pl.multiple_of((base + u) * rows, rows), rows), :] = got
         return carry
 
-    steps = boxes // 8
-    lax.fori_loop(0, steps // 2, count, 0)
+    steps = boxes // 16
+    cuts = [steps * part_of // 16 for part_of in COUNT_CUTS]
+
+    def count_part(i):
+        lax.fori_loop(cuts[i], cuts[i + 1], count, 0)
+
+    count_part(0)
 
     read_own.wait()
     box_ids = lax.broadcasted_iota(jnp.int32, (boxes, slots), 0)
-
-    def picker(g):
-        return jnp.where(lab_recv[g, 0:1, 0:slots] == box_ids, 1.0, 0.0).astype(BF)
 
     for g, k in groups:
         @pl.when(inside(-k))
         def _(g=g, k=k):
-            send_spill(g, k).wait_recv()
             send_label(g, k).wait_recv()
-            more = jnp.dot(picker(g), sp_recv[g], preferred_element_type=F32)
-            for m in range(comps):
-                own_v[m] += more[:, m * q:(m + 1) * q]
-
-    for m in range(comps):
-        win[p, OWN, m] = own_v[m].astype(BF)
+            pick[g] = jnp.where(lab_recv[g, 0:1, 0:slots] == box_ids, 1.0, 0.0).astype(BF)
+
+        @pl.when(jnp.logical_not(inside(-k)))
+        def _(g=g):
+            pick[g] = jnp.zeros((boxes, slots), BF)
 
     def up(m):
         return remote(win.at[p, OWN, m], win.at[p, LOW, m], halo_sem.at[0, m], cube=c + 1)
@@ -149,15 +165,24 @@
         return remote(win.at[owner, b, m], win.at[owner, b, m], near_sem.at[which, b, m], pair=near)
 
     for m in range(comps):
+        for g, k in groups:
+            @pl.when(inside(-k))
+            def _(g=g, k=k, m=m):
+                send_spill(g, k, m).wait_recv()
+                own_v[m] += jnp.dot(pick[g], sp_recv[g, m], preferred_element_type=F32)
+
+        win[p, OWN, m] = own_v[m].astype(BF)
+
         @pl.when(inside(1))
-        def _():
+        def _(m=m):
             up(m).start()
 
         @pl.when(inside(-1))
-        def _():
+        def _(m=m):
             down(m).start()
 
-        to_far(OWN, m).start()
+        if m < comps - 1:
+            to_far(OWN, m).start()
         to_near(OWN, m, 0).start()
 
     @pl.when(jnp.logical_not(inside(-1)))
@@ -168,7 +193,7 @@
     def _():
         win[p, HIGH] = jnp.zeros(win.shape[2:], BF)
 
-    lax.fori_loop(steps // 2, steps, count, 0)
+    count_part(1)
 
     def relay(m):
         @pl.when(inside(-1))
@@ -184,11 +209,12 @@
 
         to_far(HIGH, m).start()
         to_near(HIGH, m, 0).start()
-        to_far(OWN, m).wait_recv()
-        to_near(OWN, m, 1).start()
+        if m < comps - 1:
+            to_far(OWN, m).wait_recv()
+            to_near(OWN, m, 1).start()
 
     def pass_near(m):
-        for b in (LOW, HIGH):
+        for b in (LOW, HIGH) if m < comps - 1 else (LOW, OWN, HIGH):
             to_far(b, m).wait_recv()
             to_near(b, m, 1).start()
 
@@ -230,18 +256,37 @@
         reduce_far(m).wait_recv()
         total = part[m, :, columns(p)] + rs1_recv[m, hi].astype(F32) + rs2_recv[m].astype(F32)
         own_out[m] = total
-        field[:, m * q:(m + 1) * q] = total.astype(BF)
+        return total.astype(BF)
+
+    def send_back(g, k, m):
+        return remote(
+            rt_send.at[m, g * slots:(g + 1) * slots], rt_recv.at[m, g * slots:(g + 1) * slots],
+            rt_sem.at[g, m], cube=c - k,
+        )
+
+    def give_back(m, total):
+        rt_send[m] = jnp.dot(pick_t[...], total, preferred_element_type=F32).astype(BF)
+        for g, k in groups:
+            @pl.when(inside(-k))
+            def _(g=g, k=k):
+                send_back(g, k, m).start()
 
     relay(0)
+    to_far(OWN, comps - 1).start()
+    count_part(2)
+    relay(1)
+    pass_near(0)
+    count_part(3)
+    relay(2)
+    pass_near(1)
+    count_part(4)
+    for g, k in groups:
+        pick_t[g * slots:(g + 1) * slots, :] = jnp.transpose(pick[g].astype(F32)).astype(BF)
     for r in range(held):
         for t in range(tiles):
             cnt[r * boxes:(r + 1) * boxes, t * LANES:(t + 1) * LANES] = cnt_f[
                 pl.ds(r * tiles + t, boxes, stride=rows), :
             ].astype(BF)
-    relay(1)
-    pass_near(0)
-    relay(2)
-    pass_near(1)
     read_op.wait()
     compute(0)
     pass_near(2)
@@ -249,30 +294,19 @@
     fold(0)
     compute(2)
     fold(1)
-    finish(0)
+    give_back(0, finish(0))
     fold(2)
-    finish(1)
-    finish(2)
-
-    def send_back(g, k):
-        return remote(rt_send.at[g], rt_recv.at[g], rt_sem.at[g], cube=c - k)
-
-    for g, k in groups:
-        @pl.when(inside(-k))
-        def _(g=g, k=k):
-            rt_send[g] = lax.dot_general(
-                picker(g), field[...], (((0,), (0,)), ((), ())), preferred_element_type=F32
-            ).astype(BF)
-            send_back(g, k).start()
+    give_back(1, finish(1))
+    give_back(2, finish(2))
 
     for g, k in groups:
         rows_out = slice(g * slots, (g + 1) * slots)
 
         @pl.when(inside(k))
         def _(g=g, k=k, rows_out=rows_out):
-            send_back(g, k).wait_recv()
             for m in range(comps):
-                spill_out[m, rows_out, :] = rt_recv[g, :, m * q:(m + 1) * q].astype(F32)
+                send_back(g, k, m).wait_recv()
+                spill_out[m, rows_out, :] = rt_recv[m, rows_out, :].astype(F32)
 
         @pl.when(jnp.logical_not(inside(k)))
         def _(rows_out=rows_out):
@@ -282,12 +316,14 @@
     for g, k in groups:
         @pl.when(inside(k))
         def _(g=g, k=k):
-            send_spill(g, k).wait_send()
+            for m in range(comps):
+                send_spill(g, k, m).wait_send()
             send_label(g, k).wait_send()
 
         @pl.when(inside(-k))
         def _(g=g, k=k):
-            send_back(g, k).wait_send()
+            for m in range(comps):
+                send_back(g, k, m).wait_send()
 
     for m in range(comps):
         @pl.when(inside(1))
@@ -318,23 +354,27 @@
     width = -(-sources.shape[1] // LANES) * LANES
     dma = pltpu.SemaphoreType.DMA
     vmem = pl.BlockSpec(memory_space=pltpu.VMEM)
-    anywhere = pl.BlockSpec(memory_space=pl.ANY)
+    anywhere = pl.BlockSpec(memory_space=pltpu.HBM)
     return pl.pallas_call(
         functools.partial(kernel, cubes, pairs),
         out_shape=(
             jax.ShapeDtypeStruct((comps, boxes, q), F32),
             jax.ShapeDtypeStruct((comps, spills, q), F32),
         ),
-        in_specs=[anywhere, anywhere, vmem, vmem, vmem, anywhere],
+        in_specs=[anywhere] * 6,
         out_specs=(vmem, vmem),
         scratch_shapes=[
             pltpu.VMEM((comps, boxes, q), F32),
             pltpu.VMEM((comps, spills, q), F32),
             pltpu.VMEM((held, coeffs, outs), BF),
+            pltpu.VMEM((1, spills), jnp.int32),
+            pltpu.VMEM(sources.shape[::-1], jnp.int32),
+            pltpu.VMEM(sources.shape[::-1], jnp.int32),
             pltpu.VMEM((groups, 8, LANES), jnp.int32),
             pltpu.VMEM((groups, 8, LANES), jnp.int32),
-            pltpu.VMEM((groups, slots, comps * q), BF),
-            pltpu.VMEM((groups, slots, comps * q), BF),
+            pltpu.VMEM((groups, comps, slots, q), BF),
+            pltpu.VMEM((groups, comps, slots, q), BF),
+            pltpu.VMEM((width, boxes), F32),
             pltpu.VMEM((boxes, width), F32),
             pltpu.VMEM((boxes, width), F32),
             pltpu.VMEM((boxes * rows, LANES), F32),
@@ -346,24 +386,25 @@
             pltpu.VMEM((comps, pairs // 2, boxes, q), BF),
             pltpu.VMEM((comps, boxes, q), BF),
             pltpu.VMEM((comps, boxes, q), BF),
-            pltpu.VMEM((boxes, comps * q), BF),
-            pltpu.VMEM((groups, slots, comps * q), BF),
-            pltpu.VMEM((groups, slots, comps * q), BF),
-            dma((3,)),
+            pltpu.VMEM((groups, boxes, slots), BF),
+            pltpu.VMEM((spills, boxes), BF),
+            pltpu.VMEM((comps, spills, q), BF),
+            pltpu.VMEM((comps, spills, q), BF),
+            dma((6,)),
             dma((groups, 2)),
-            dma((groups, 2)),
+            dma((groups, comps, 2)),
             dma((2, comps, 2)),
             dma((3, comps, 2)),
             dma((2, 3, comps, 2)),
             dma((comps, 2)),
             dma((comps, 2)),
-            dma((groups, 2)),
+            dma((groups, comps, 2)),
         ],
         compiler_params=pltpu.CompilerParams(
-            collective_id=0, has_side_effects=True, vmem_limit_bytes=40 * 1024 * 1024
+            collective_id=0, has_side_effects=True, vmem_limit_bytes=52 * 1024 * 1024
         ),
         name="far_field",
-    )(own_partial, spill_partial, spill_box.reshape(1, spills), sources, reflections, operators)
+    )(own_partial, spill_partial, spill_box.reshape(1, spills), sources.T, reflections.T, operators)
 
 
 def solution(mesh):

time: 50.5 us -> 45.3 us (0.90)
  local copies, waits for them, and re-layouts: 8.68 us -> 4.02 us
    unnamed x12 -> x8, local copies, waits for them, and re-layouts: 8.68 us -> 4.02 us
where the time goes in v2:
time: 45.3 us; the launch traced here: 45.1 us
  Pallas kernels  40.4 us (89%)
  local copies, waits for them, and re-layouts  4.02 us (9%)
  between operations  0.65 us (1%)
    pallas_call x1, Pallas kernels, on_device(): pl.pallas_call(functools.partial(kernel, cubes, pairs), out_shape=(jax.Sh...  40.4 us
    unnamed x8, local copies, waits for them, and re-layouts  4.02 us

profile of v2, /device:TPU:0, one launch (start us, length us, event | category | flops | bytes accessed | tf_op | source)
XLA Modules:
  0.0 45.1 jit_solution(13427686938304509340)
XLA Ops:
  0.6 0.0 copy-start
  0.6 0.9 %copy-done = s32[256,189]{0,1:T(8,128)S(1)} copy-done((s32[256,189]{0,1:T(8,128)S(1)}, s32[256,189]{0,1:T(8,128)}, u32[]{:S(2)}) %copy-start) | copy-done | bytes 193560
  1.6 0.0 copy-start.1
  1.6 0.9 %copy-done.1 = s32[256,189]{0,1:T(8,128)S(1)} copy-done((s32[256,189]{0,1:T(8,128)S(1)}, s32[256,189]{0,1:T(8,128)}, u32[]{:S(2)}) %copy-start.1) | copy-done | bytes 193560
  2.5 0.0 copy-start.2
  2.5 0.7 %copy-done.2 = s32[256]{0:T(256)S(1)} copy-done((s32[256]{0:T(256)S(1)}, s32[256]{0:T(256)}, u32[]{:S(2)}) %copy-start.2) | copy-done | bytes 1048
  3.2 40.4 %far_field.1 = (f32[3,256,128]{2,1,0:T(8,128)S(1)}, f32[3,256,128]{2,1,0:T(8,128)S(1)}) custom-call(f32[3,256,512]{2,1,0:T(8,128)} %own_hbm.1, f32[3,256,512]{2,1,0:T(8,128)} %spill_hbm.1, s32[1,256]{1,0:T(1,128)S(1)} %bitcast.5, s32[189,256]{1,0:T(8,128)S(1)} %bitcast.3, s32[189,256]{1,0:T(8,128)S(1)} %bitcast.4, bf16[4,512,512]{2,1,0:T(8,128)(2,1)} %op_hbm.1), custom_call_target="tpu_custom_call" | custom-call | tf_op jit(solution)/shard_map/far_field/pallas_call | solution.py:358
  43.6 0.7 %copy.10 = f32[3,256,128]{2,1,0:T(8,128)} copy(f32[3,256,128]{2,1,0:T(8,128)S(1)} %get-tuple-element.4) | data formatting | bytes 786432
  44.3 0.7 %copy.11 = f32[3,256,128]{2,1,0:T(8,128)} copy(f32[3,256,128]{2,1,0:T(8,128)S(1)} %get-tuple-element.5) | data formatting | bytes 786432
Async XLA Ops:
  0.6 0.9 %copy-start = (s32[256,189]{0,1:T(8,128)S(1)}, s32[256,189]{0,1:T(8,128)}, u32[]{:S(2)}) copy-start(s32[256,189]{0,1:T(8,128)} %param.9) | copy-start | bytes 580612
  1.6 0.9 %copy-start.1 = (s32[256,189]{0,1:T(8,128)S(1)}, s32[256,189]{0,1:T(8,128)}, u32[]{:S(2)}) copy-start(s32[256,189]{0,1:T(8,128)} %param.10) | copy-start | bytes 580612
  2.5 0.7 %copy-start.2 = (s32[256]{0:T(256)S(1)}, s32[256]{0:T(256)}, u32[]{:S(2)}) copy-start(s32[256]{0:T(256)} %param.8) | copy-start | bytes 3076
